TPU v7x, 32 devices: a whole 2x2x4 slice. The times are simulated.
32 devices in a mesh: gx: 8 (over y, x, core), gy: 4 (over z).
Axes of the slice: x: 2, y: 2, z: 4, core: 2. Of those that a mesh axis runs over, the one named last changes fastest.
Arguments:
- state: float32 [9, 56, 4096], P(None, None, ('gx', 'gy')), may hold values from -6 to 6
- star_matrices: float32 [3, 9, 9, 4096], P(None, None, None, ('gx', 'gy')), may hold values from -1.25 to 1.25
- stiffness: float32 [3, 56, 56], replicated, may hold values from -0.75 to 0.75
- face_project: float32 [4, 21, 56], replicated, may hold values from -0.75 to 0.75
- flux_inner: float32 [9, 9], replicated, may hold values from -2 to 2
- flux_outer: float32 [9, 9], replicated, may hold values from -2 to 2
- rate_level: int32 [4096], P(('gx', 'gy')), may hold values from 0 to 2
- neighbour: int32 [4, 4096], P(None, ('gx', 'gy')), may hold values from 0 to 511
- send_slots: int32 [4, 8192], P(None, ('gx', 'gy')), may hold values from 0 to 511
- receive_slots: int32 [4, 8192], P(None, ('gx', 'gy')), may hold values from 0 to 511
- fault_faces: int32 [2048], P(('gx', 'gy')), may hold values from 0 to 511, as said below
- slip_flags: int32 [2048], P(('gx', 'gy')), may hold values 0 or 1
Outputs:
- updated: float32 [9, 56, 4096], P(None, None, ('gx', 'gy'))
Inputs may be any that keep to these rules, and one draw needn't show every extreme that they name: `neighbour`: local face indices f * 128 + e of the device's own elements. `send_slots`: local face indices of the sending device's own elements. `receive_slots`: local face indices of the receiving device's own elements; two slots may act on one face. `fault_faces`: local face indices of the device's own elements, distinct within one device.
All inputs are finite; a program needn't handle non-finite values. No bound on the sum of `slip_flags` on one device may be relied on, other than what follows from the above.
Results may differ from a plain program's by a relative error of at most 0.0003.
Values sent between devices are 32-bit elements; how exact they have to be, the bound alone decides.
A program may use at most 64 MiB of HBM per device.

v0:
```python
import jax
import jax.numpy as jnp
from jax import lax
from jax.sharding import PartitionSpec as P

FIELDS = 9
FACE_MODES = 21
ORDER = 6


coarse_dt = 2.0
slip_keep = 0.3


def shifted(value, axis, steps):
    count = lax.axis_size(axis)
    first, last = (max(0, -steps), min(count, count - steps))
    return lax.ppermute(value, axis, [(source, source + steps) for source in range(first, last)])


def taylor_terms(rate_level):
    step_size = coarse_dt * jnp.exp2(-rate_level.astype(jnp.float32))
    terms = []
    factor = step_size
    for degree in range(ORDER):
        terms.append(factor)
        factor = factor * step_size / (degree + 2.0)
    return terms


def star_apply(star_matrices, modal):
    return jnp.sum(star_matrices[:, :, :, None, :] * modal[:, :, None, :, :], axis=(0, 1))


def derive(current, star_matrices, stiffness):
    modal = jnp.einsum("dmn,qne->dqme", stiffness, current, precision=lax.Precision.HIGHEST)
    return -star_apply(star_matrices, modal)


def volume_term(integral, star_matrices, stiffness):
    modal = jnp.einsum("dnm,qne->dqme", stiffness, integral, precision=lax.Precision.HIGHEST)
    return star_apply(star_matrices, modal)


def on_faces(field, face_project):
    faces = jnp.einsum("fjn,qne->qjfe", face_project, field, precision=lax.Precision.HIGHEST)
    return faces.reshape(FIELDS * FACE_MODES, -1)


def lift_faces(face_terms, face_project):
    shaped = face_terms.reshape(FIELDS, FACE_MODES, 4, -1)
    return jnp.einsum("fjm,qjfe->qme", face_project, shaped, precision=lax.Precision.HIGHEST)


def apply_flux(matrix, face_terms):
    shaped = face_terms.reshape(FIELDS, FACE_MODES, -1)
    mixed = jnp.einsum("qp,qjx->pjx", matrix, shaped, precision=lax.Precision.HIGHEST)
    return mixed.reshape(FIELDS * FACE_MODES, -1)


def keep_mask(fault_faces, slip_flags, count):
    slide = jnp.zeros((4 * count,), jnp.float32).at[fault_faces].set(slip_flags.astype(jnp.float32))
    fields = jnp.arange(FIELDS)
    shear = ((fields >= 3) & (fields < 6)).astype(jnp.float32)
    keep = 1.0 - (1.0 - slip_keep) * shear[:, None] * slide[None, :]
    return jnp.repeat(keep, FACE_MODES, axis=0)


def move_stack(piece, direction):
    if direction < 2:
        return shifted(piece, "gx", 1 - 2 * direction)
    return shifted(piece, "gy", 1 - 2 * (direction - 2))


def weigh_stack(terms, stack):
    arrived = terms[0][None, :] * stack[0]
    for degree in range(1, ORDER):
        arrived = arrived + terms[degree][None, :] * stack[degree]
    return arrived


def shards(
    state,
    star_matrices,
    stiffness,
    face_project,
    flux_inner,
    flux_outer,
    rate_level,
    neighbour,
    send_slots,
    receive_slots,
    fault_faces,
    slip_flags,
):
    count = state.shape[-1]
    terms = taylor_terms(rate_level)
    current = state
    integral = terms[0] * state
    outer = jnp.zeros((FIELDS * FACE_MODES, 4 * count), jnp.float32)
    flat_neighbour = neighbour.reshape(-1)
    sent = []
    for degree in range(ORDER):
        if degree > 0:
            current = derive(current, star_matrices, stiffness)
            integral = integral + terms[degree] * current
        faces = on_faces(current, face_project)
        outer = outer + jnp.tile(terms[degree], 4)[None, :] * faces[:, flat_neighbour]
        sent.append(faces[:, send_slots])
    stacks = jnp.stack(sent)
    target_level = rate_level[receive_slots % count]
    for direction in range(4):
        incoming = move_stack(stacks[:, :, direction, :], direction)
        arrived = weigh_stack([part[direction] for part in taylor_terms(target_level)], incoming)
        outer = outer.at[:, receive_slots[direction]].add(arrived)
    inner = on_faces(integral, face_project)
    keep = keep_mask(fault_faces, slip_flags, count)
    flux = apply_flux(flux_inner, inner) + apply_flux(flux_outer, outer * keep)
    return state + volume_term(integral, star_matrices, stiffness) + lift_faces(flux, face_project)


def solution(mesh):
    placed = (
        P(None, None, ("gx", "gy")),
        P(None, None, None, ("gx", "gy")),
        P(),
        P(),
        P(),
        P(),
        P(("gx", "gy")),
        P(None, ("gx", "gy")),
        P(None, ("gx", "gy")),
        P(None, ("gx", "gy")),
        P(("gx", "gy")),
        P(("gx", "gy")),
    )
    return jax.shard_map(
        shards, mesh=mesh, in_specs=placed, out_specs=P(None, None, ("gx", "gy")), check_vma=False
    )
```

profile of v0, /device:TPU:1, one launch (start us, length us, event | category | flops | bytes accessed | tf_op | source)
XLA Modules:
  0.0 142.1 jit_solution(9492538881873762142)
XLA Ops:
  0.0 1.0 copy.182
  1.0 1.8 %convolution_bitcast_fusion.5 = f32[3,9,56,128]{3,2,0,1:T(8,128)S(1)} fusion(f32[9,56,128]{2,1,0:T(8,128)} %param.12, f32[3,56,56]{2,1,0:T(8,128)S(1)} %copy-done), kind=kOutput, calls=%fused_computation.29 | convolution fusion | flops 130056192 | bytes 1069824 | tf_op jit(solution)/shard_map/dmn,qne->dqme/dot_general | solution.py:36
  13.6 1.2 copy.211
  15.8 1.2 copy.208
  17.9 1.2 copy.205
  20.1 1.2 copy.202
  22.2 1.4 copy.199
  24.6 1.2 copy.196
  25.8 4.7 %gather_fusion.7 = f32[1024,189]{1,0:T(8,128)} fusion(f32[189,512]{0,1:T(8,128)S(1)} %copy.196, s32[1024]{0:T(1024)S(1)} %broadcast_clamp_fusion.1), kind=kCustom, calls=%fused_computation.7 | custom fusion | bytes 1552384 | tf_op jit(solution)/shard_map/gather | solution.py:109
  30.5 2.4 %copy.213 = f32[4,256,189]{1,2,0:T(8,128)} copy(f32[4,256,189]{2,1,0:T(8,128)} %bitcast.440) | data formatting | bytes 1548288 | tf_op jit(solution)/shard_map/gather | solution.py:109
  32.9 2.0 %bitcast_dynamic-update-slice_fusion.5 = f32[6,189,4,256]{3,1,0,2:T(8,128)} fusion(f32[4,256,189]{1,2,0:T(8,128)} %copy.213), kind=kLoop, calls=%fused_computation.50 | loop fusion | bytes 1560576
  35.0 4.7 %gather_fusion.8 = f32[1024,189]{1,0:T(8,128)} fusion(f32[189,512]{0,1:T(8,128)S(1)} %copy.199, s32[1024]{0:T(1024)S(1)} %broadcast_clamp_fusion.1), kind=kCustom, calls=%fused_computation.8 | custom fusion | bytes 1552384 | tf_op jit(solution)/shard_map/gather | solution.py:109
  39.7 2.4 %copy.215 = f32[4,256,189]{1,2,0:T(8,128)} copy(f32[4,256,189]{2,1,0:T(8,128)} %bitcast.441) | data formatting | bytes 1548288 | tf_op jit(solution)/shard_map/gather | solution.py:109
  42.1 4.7 %gather_fusion.9 = f32[1024,189]{1,0:T(8,128)} fusion(f32[189,512]{0,1:T(8,128)S(1)} %copy.202, s32[1024]{0:T(1024)S(1)} %broadcast_clamp_fusion.1), kind=kCustom, calls=%fused_computation.9 | custom fusion | bytes 1552384 | tf_op jit(solution)/shard_map/gather | solution.py:109
  46.9 2.4 %copy.217 = f32[4,256,189]{1,2,0:T(8,128)} copy(f32[4,256,189]{2,1,0:T(8,128)} %bitcast.442) | data formatting | bytes 1548288 | tf_op jit(solution)/shard_map/gather | solution.py:109
  49.3 4.7 %gather_fusion.10 = f32[1024,189]{1,0:T(8,128)} fusion(f32[189,512]{0,1:T(8,128)S(1)} %copy.205, s32[1024]{0:T(1024)S(1)} %broadcast_clamp_fusion.1), kind=kCustom, calls=%fused_computation.10 | custom fusion | bytes 1552384 | tf_op jit(solution)/shard_map/gather | solution.py:109
  54.0 2.4 %copy.219 = f32[4,256,189]{1,2,0:T(8,128)} copy(f32[4,256,189]{2,1,0:T(8,128)} %bitcast.443) | data formatting | bytes 1548288 | tf_op jit(solution)/shard_map/gather | solution.py:109
  56.4 4.7 %gather_fusion.11 = f32[1024,189]{1,0:T(8,128)} fusion(f32[189,512]{0,1:T(8,128)S(1)} %copy.208, s32[1024]{0:T(1024)S(1)} %broadcast_clamp_fusion.1), kind=kCustom, calls=%fused_computation.11 | custom fusion | bytes 1552384 | tf_op jit(solution)/shard_map/gather | solution.py:109
  61.2 2.5 %copy.221 = f32[4,256,189]{1,2,0:T(8,128)} copy(f32[4,256,189]{2,1,0:T(8,128)} %bitcast.444) | data formatting | bytes 1548288 | tf_op jit(solution)/shard_map/gather | solution.py:109
  63.6 4.7 %gather_fusion.12 = f32[1024,189]{1,0:T(8,128)} fusion(f32[189,512]{0,1:T(8,128)S(1)} %copy.211, s32[1024]{0:T(1024)S(1)} %broadcast_clamp_fusion.1), kind=kCustom, calls=%fused_computation.12 | custom fusion | bytes 1552384 | tf_op jit(solution)/shard_map/gather | solution.py:109
  68.4 2.4 %copy.223 = f32[4,256,189]{1,2,0:T(8,128)} copy(f32[4,256,189]{2,1,0:T(8,128)} %bitcast.439) | data formatting | bytes 1548288 | tf_op jit(solution)/shard_map/gather | solution.py:109
  70.8 2.2 %bitcast_dynamic-update-slice_fusion.4 = f32[6,189,4,256]{3,1,0,2:T(8,128)} fusion(f32[6,189,4,256]{3,1,0,2:T(8,128)} %bitcast_dynamic-update-slice_fusion.5, f32[4,256,189]{1,2,0:T(8,128)} %copy.215), kind=kLoop, calls=%fused_computation.49 | loop fusion | bytes 1572864
  73.0 2.1 %bitcast_dynamic-update-slice_fusion.3 = f32[6,189,4,256]{3,1,0,2:T(8,128)} fusion(f32[6,189,4,256]{3,1,0,2:T(8,128)} %bitcast_dynamic-update-slice_fusion.4, f32[4,256,189]{1,2,0:T(8,128)} %copy.217), kind=kLoop, calls=%fused_computation.48 | loop fusion | bytes 1572864
  75.1 2.1 %bitcast_dynamic-update-slice_fusion.2 = f32[6,189,4,256]{3,1,0,2:T(8,128)} fusion(f32[6,189,4,256]{3,1,0,2:T(8,128)} %bitcast_dynamic-update-slice_fusion.3, f32[4,256,189]{1,2,0:T(8,128)} %copy.219), kind=kLoop, calls=%fused_computation.47 | loop fusion | bytes 1572864
  79.0 4.7 %slice_bitcast_fusion = (f32[6,189,256]{2,1,0:T(8,128)}, f32[6,189,256]{2,1,0:T(8,128)}, f32[6,189,256]{2,1,0:T(8,128)}, f32[6,189,256]{2,1,0:T(8,128)}) fusion(f32[6,189,4,256]{3,1,0,2:T(8,128)} %bitcast_dynamic-update-slice_fusion), kind=kLoop, calls=%fused_computation.39 | loop fusion | bytes 9289728 | tf_op jit(solution)/shard_map/squeeze | solution.py:113
  83.7 4.5 %collective-permute-start = (f32[6,189,256]{2,1,0:T(8,128)}, f32[6,189,256]{2,1,0:T(8,128)}, u32[]{:S(2)}, u32[]{:S(2)}) collective-permute-start(f32[6,189,256]{2,1,0:T(8,128)} %get-tuple-element.10), channel_id=1, source_target_pairs={{0,4},{4,8},{8,12},{12,16},{16,20},{20,24},{24,28},{1,5},{5,9},{9,... | collective-permute-start | bytes 3483656 | tf_op jit(solution)/shard_map/ppermute | solution.py:18
  88.2 1.9 %collective-permute-start.1 = (f32[6,189,256]{2,1,0:T(8,128)}, f32[6,189,256]{2,1,0:T(8,128)}, u32[]{:S(2)}, u32[]{:S(2)}) collective-permute-start(f32[6,189,256]{2,1,0:T(8,128)} %get-tuple-element.9), channel_id=1, source_target_pairs={{4,0},{8,4},{12,8},{16,12},{20,16},{24,20},{28,24},{5,1},{9,5},{13... | collective-permute-start | bytes 3483656 | tf_op jit(solution)/shard_map/ppermute | solution.py:18
  90.2 4.2 %collective-permute-start.2 = (f32[6,189,256]{2,1,0:T(8,128)}, f32[6,189,256]{2,1,0:T(8,128)}, u32[]{:S(2)}, u32[]{:S(2)}) collective-permute-start(f32[6,189,256]{2,1,0:T(8,128)} %get-tuple-element.8), channel_id=1, source_target_pairs={{0,1},{1,2},{2,3},{4,5},{5,6},{6,7},{8,9},{9,10},{10,11},{12,13},{... | collective-permute-start | bytes 3483656 | tf_op jit(solution)/shard_map/ppermute | solution.py:18
  94.4 1.3 collective-permute-start.3
  95.8 2.2 %gather_fusion.5 = f32[512,189]{1,0:T(8,128)} fusion(f32[189,512]{0,1:T(8,128)S(1)} %copy.211, s32[1024]{0:T(1024)S(1)} %get-tuple-element.48), kind=kCustom, calls=%fused_computation.5 | custom fusion | bytes 776192 | tf_op jit(solution)/shard_map/gather | solution.py:108
  98.0 2.2 %gather_fusion.4 = f32[512,189]{1,0:T(8,128)} fusion(f32[189,512]{0,1:T(8,128)S(1)} %copy.208, s32[1024]{0:T(1024)S(1)} %get-tuple-element.48), kind=kCustom, calls=%fused_computation.4 | custom fusion | bytes 776192 | tf_op jit(solution)/shard_map/gather | solution.py:108
  100.2 2.2 %gather_fusion.3 = f32[512,189]{1,0:T(8,128)} fusion(f32[189,512]{0,1:T(8,128)S(1)} %copy.205, s32[1024]{0:T(1024)S(1)} %get-tuple-element.48), kind=kCustom, calls=%fused_computation.3 | custom fusion | bytes 776192 | tf_op jit(solution)/shard_map/gather | solution.py:108
  102.5 2.2 %gather_fusion.2 = f32[512,189]{1,0:T(8,128)} fusion(f32[189,512]{0,1:T(8,128)S(1)} %copy.202, s32[1024]{0:T(1024)S(1)} %get-tuple-element.48), kind=kCustom, calls=%fused_computation.2 | custom fusion | bytes 776192 | tf_op jit(solution)/shard_map/gather | solution.py:108
  104.7 2.2 %gather_fusion.1 = f32[512,189]{1,0:T(8,128)} fusion(f32[189,512]{0,1:T(8,128)S(1)} %copy.199, s32[1024]{0:T(1024)S(1)} %get-tuple-element.48), kind=kCustom, calls=%fused_computation.1 | custom fusion | bytes 776192 | tf_op jit(solution)/shard_map/gather | solution.py:108
  107.0 2.2 %gather_fusion = f32[512,189]{1,0:T(8,128)} fusion(f32[189,512]{0,1:T(8,128)S(1)} %copy.196, s32[1024]{0:T(1024)S(1)} %get-tuple-element.48), kind=kCustom, calls=%fused_computation | custom fusion | bytes 776192 | tf_op jit(solution)/shard_map/gather | solution.py:108
  109.3 6.6 %gather_fusion.6 = s32[1024]{0:T(1024)S(1)} fusion(s32[128]{0:T(128)S(1)} %copy-done.1, s32[1024]{0:T(1024)S(1)} %get-tuple-element.49), kind=kCustom, calls=%fused_computation.6 | custom fusion | bytes 12288 | tf_op jit(solution)/shard_map/gather | solution.py:111
  118.0 1.0 scatter_custom_fusion.4
  121.5 2.2 %add_bitcast_fusion = f32[189,512]{0,1:T(8,128)S(1)} fusion(f32[512,189]{1,0:T(8,128)S(1)} %copy-done.17, f32[512,189]{1,0:T(8,128)} %gather_fusion.4, f32[512,189]{1,0:T(8,128)} %gather_fusion.3, f32[512,189]{1,0:T(8,128)} %gather_fusion.2, f32[512,189]{1,0:T(8,128)} %gather_fusion.1, f32[512,189]{1,0:T(8,128)} %gather_fusion, ...), kind=kLoop, calls=%fused_computation.52 | loop fusion | flops 1064448 | bytes 2721792 | tf_op jit(solution)/shard_map/add | solution.py:108
  123.6 1.4 %fusion.64 = f32[256,189]{0,1:T(8,128)S(1)} fusion(f32[6,189,256]{2,1,0:T(8,128)} %collective-permute-done, f32[256]{0:T(256)S(1)} %get-tuple-element.34, f32[256]{0:T(256)S(1)} %bitcast.482, f32[256]{0:T(256)S(1)} %bitcast.484, f32[256]{0:T(256)S(1)} %bitcast.485, f32[256]{0:T(256)S(1)} %bitcast.487, f32[256]{0:T(256)S(1)} %bitcast.489), kind=kLoop, calls=%fused_computation.134 | loop fusion | flops 532224 | bytes 1360896 | tf_op jit(solution)/shard_map/add | solution.py:78
  125.2 1.4 %fusion.52 = f32[256,189]{0,1:T(8,128)S(1)} fusion(f32[6,189,256]{2,1,0:T(8,128)} %collective-permute-done.1, f32[256]{0:T(256)S(1)} %get-tuple-element.33, f32[256]{0:T(256)S(1)} %bitcast.477, f32[256]{0:T(256)S(1)} %bitcast.479, f32[256]{0:T(256)S(1)} %bitcast.481, f32[256]{0:T(256)S(1)} %bitcast.483, f32[256]{0:T(256)S(1)} %bitcast.488), kind=kLoop, calls=%fused_computation.116 | loop fusion | flops 532224 | bytes 1360896 | tf_op jit(solution)/shard_map/add | solution.py:78
  126.8 1.4 %fusion.40 = f32[256,189]{0,1:T(8,128)S(1)} fusion(f32[6,189,256]{2,1,0:T(8,128)} %collective-permute-done.2, f32[256]{0:T(256)S(1)} %get-tuple-element.32, f32[256]{0:T(256)S(1)} %bitcast.474, f32[256]{0:T(256)S(1)} %bitcast.475, f32[256]{0:T(256)S(1)} %bitcast.476, f32[256]{0:T(256)S(1)} %bitcast.478, f32[256]{0:T(256)S(1)} %bitcast.486), kind=kLoop, calls=%fused_computation.98 | loop fusion | flops 532224 | bytes 1360896 | tf_op jit(solution)/shard_map/add | solution.py:78
  128.4 1.4 %fusion.28 = f32[256,189]{0,1:T(8,128)S(1)} fusion(f32[6,189,256]{2,1,0:T(8,128)} %collective-permute-done.3, f32[256]{0:T(256)S(1)} %get-tuple-element.31, f32[256]{0:T(256)S(1)} %bitcast.470, f32[256]{0:T(256)S(1)} %bitcast.471, f32[256]{0:T(256)S(1)} %bitcast.472, f32[256]{0:T(256)S(1)} %bitcast.473, f32[256]{0:T(256)S(1)} %bitcast.480), kind=kLoop, calls=%fused_computation.80 | loop fusion | flops 532224 | bytes 1360896 | tf_op jit(solution)/shard_map/add | solution.py:78
  130.6 2.2 %scatter_fusion = f32[189,512]{0,1:T(8,128)S(1)} fusion(f32[189,512]{0,1:T(8,128)S(1)} %add_bitcast_fusion, s32[256]{0:T(256)S(1)} %bitcast.469, f32[256,189]{1,0:T(8,128)S(1)} %copy.224), kind=kCustom, calls=%fused_computation.13 | custom fusion | flops 48384 | bytes 581632 | tf_op jit(solution)/shard_map/scatter-add | solution.py:115
  132.8 2.2 %scatter_fusion.1 = f32[189,512]{0,1:T(8,128)S(1)} fusion(f32[189,512]{0,1:T(8,128)S(1)} %scatter_fusion, s32[256]{0:T(256)S(1)} %bitcast.468, f32[256,189]{1,0:T(8,128)S(1)} %copy.225), kind=kCustom, calls=%fused_computation.14 | custom fusion | flops 48384 | bytes 581632 | tf_op jit(solution)/shard_map/scatter-add | solution.py:115
  135.0 2.2 %scatter_fusion.2 = f32[189,512]{0,1:T(8,128)S(1)} fusion(f32[189,512]{0,1:T(8,128)S(1)} %scatter_fusion.1, s32[256]{0:T(256)S(1)} %bitcast.467, f32[256,189]{1,0:T(8,128)S(1)} %copy.226), kind=kCustom, calls=%fused_computation.15 | custom fusion | flops 48384 | bytes 581632 | tf_op jit(solution)/shard_map/scatter-add | solution.py:115
  137.2 2.2 %scatter_fusion.3 = f32[189,512]{0,1:T(8,128)S(1)} fusion(f32[189,512]{0,1:T(8,128)S(1)} %scatter_fusion.2, s32[256]{0:T(256)S(1)} %bitcast.466, f32[256,189]{1,0:T(8,128)S(1)} %copy-done.19), kind=kCustom, calls=%fused_computation.16 | custom fusion | flops 48384 | bytes 581632 | tf_op jit(solution)/shard_map/scatter-add | solution.py:115
  139.7 1.1 fusion
  140.9 1.1 fusion.1
  (136 shorter events, 23.4 us)
Async XLA Ops:
  0.0 1.0 copy-start
  2.8 6.1 %copy-start.12 = (f32[4,21,56]{2,0,1:T(4,128)S(1)}, f32[4,21,56]{2,0,1:T(4,128)}, u32[]{:S(2)}) copy-start(f32[4,21,56]{2,0,1:T(4,128)} %param.15) | copy-start | bytes 56452
  3.4 6.9 %copy-start.4 = (f32[9,56,128]{2,1,0:T(8,128)}, f32[9,56,128]{2,1,0:T(8,128)S(1)}, u32[]{:S(2)}) copy-start(f32[9,56,128]{2,1,0:T(8,128)S(1)} %multiply_reduce_fusion.5) | copy-start | bytes 774148
  5.0 6.5 %copy-start.6 = (f32[9,56,128]{2,1,0:T(8,128)}, f32[9,56,128]{2,1,0:T(8,128)S(1)}, u32[]{:S(2)}) copy-start(f32[9,56,128]{2,1,0:T(8,128)S(1)} %multiply_reduce_fusion.4) | copy-start | bytes 774148
  5.0 5.9 %copy-start.2 = (f32[9,56,128]{2,1,0:T(8,128)S(1)}, f32[9,56,128]{2,1,0:T(8,128)}, u32[]{:S(2)}) copy-start(f32[9,56,128]{2,1,0:T(8,128)} %param.12) | copy-start | bytes 774148
  6.5 6.3 %copy-start.8 = (f32[9,56,128]{2,1,0:T(8,128)}, f32[9,56,128]{2,1,0:T(8,128)S(1)}, u32[]{:S(2)}) copy-start(f32[9,56,128]{2,1,0:T(8,128)S(1)} %multiply_reduce_fusion.3) | copy-start | bytes 774148
  8.0 5.6 %copy-start.10 = (f32[9,56,128]{2,1,0:T(8,128)}, f32[9,56,128]{2,1,0:T(8,128)S(1)}, u32[]{:S(2)}) copy-start(f32[9,56,128]{2,1,0:T(8,128)S(1)} %multiply_reduce_fusion.2) | copy-start | bytes 774148
  12.1 1.5 %copy-start.15 = (f32[9,56,128]{2,1,0:T(8,128)}, f32[9,56,128]{2,1,0:T(8,128)S(1)}, u32[]{:S(2)}) copy-start(f32[9,56,128]{2,1,0:T(8,128)S(1)} %multiply_reduce_fusion.1) | copy-start | bytes 774148
  19.2 6.5 %copy-start.23 = (s32[4,256]{1,0:T(4,128)S(1)}, s32[4,256]{1,0:T(4,128)}, u32[]{:S(2)}) copy-start(s32[4,256]{1,0:T(4,128)} %param.20) | copy-start | bytes 12292
  70.8 6.3 %copy-start.13 = (f32[4,256,189]{1,2,0:T(8,128)S(1)}, f32[4,256,189]{1,2,0:T(8,128)}, u32[]{:S(2)}) copy-start(f32[4,256,189]{1,2,0:T(8,128)} %copy.221) | copy-start | bytes 2322436
  70.8 7.3 %copy-start.14 = (f32[4,256,189]{1,2,0:T(8,128)S(1)}, f32[4,256,189]{1,2,0:T(8,128)}, u32[]{:S(2)}) copy-start(f32[4,256,189]{1,2,0:T(8,128)} %copy.223) | copy-start | bytes 2322436
  79.0 16.7 %copy-start.24 = (s32[4,128]{1,0:T(4,128)S(1)}, s32[4,128]{1,0:T(4,128)}, u32[]{:S(2)}) copy-start(s32[4,128]{1,0:T(4,128)} %param.19) | copy-start | bytes 6148
  79.0 16.7 %copy-start.20 = (s32[4,256]{1,0:T(4,128)S(1)}, s32[4,256]{1,0:T(4,128)}, u32[]{:S(2)}) copy-start(s32[4,256]{1,0:T(4,128)} %param.21) | copy-start | bytes 12292
  83.7 39.9 %collective-permute-start = (f32[6,189,256]{2,1,0:T(8,128)}, f32[6,189,256]{2,1,0:T(8,128)}, u32[]{:S(2)}, u32[]{:S(2)}) collective-permute-start(f32[6,189,256]{2,1,0:T(8,128)} %get-tuple-element.10), channel_id=1, source_target_pairs={{0,4},{4,8},{8,12},{12,16},{16,20},{20,24},{24,28},{1,5},{5,9},{9,... | collective-permute-start | bytes 3483656 | tf_op jit(solution)/shard_map/ppermute | solution.py:18
  88.2 36.9 %collective-permute-start.1 = (f32[6,189,256]{2,1,0:T(8,128)}, f32[6,189,256]{2,1,0:T(8,128)}, u32[]{:S(2)}, u32[]{:S(2)}) collective-permute-start(f32[6,189,256]{2,1,0:T(8,128)} %get-tuple-element.9), channel_id=1, source_target_pairs={{4,0},{8,4},{12,8},{16,12},{20,16},{24,20},{28,24},{5,1},{9,5},{13... | collective-permute-start | bytes 3483656 | tf_op jit(solution)/shard_map/ppermute | solution.py:18
  90.2 36.6 %collective-permute-start.2 = (f32[6,189,256]{2,1,0:T(8,128)}, f32[6,189,256]{2,1,0:T(8,128)}, u32[]{:S(2)}, u32[]{:S(2)}) collective-permute-start(f32[6,189,256]{2,1,0:T(8,128)} %get-tuple-element.8), channel_id=1, source_target_pairs={{0,1},{1,2},{2,3},{4,5},{5,6},{6,7},{8,9},{9,10},{10,11},{12,13},{... | collective-permute-start | bytes 3483656 | tf_op jit(solution)/shard_map/ppermute | solution.py:18
  94.4 33.9 %collective-permute-start.3 = (f32[6,189,256]{2,1,0:T(8,128)}, f32[6,189,256]{2,1,0:T(8,128)}, u32[]{:S(2)}, u32[]{:S(2)}) collective-permute-start(f32[6,189,256]{2,1,0:T(8,128)} %get-tuple-element.7), channel_id=1, source_target_pairs={{1,0},{2,1},{3,2},{5,4},{6,5},{7,6},{9,8},{10,9},{11,10},{13,12},{... | collective-permute-start | bytes 3483656 | tf_op jit(solution)/shard_map/ppermute | solution.py:18
  102.5 6.7 %copy-start.1 = (s32[128]{0:T(128)S(1)}, s32[128]{0:T(128)}, u32[]{:S(2)}) copy-start(s32[128]{0:T(128)} %param.18) | copy-start | bytes 1540
  106.9 9.0 %copy-start.3 = (f32[9,56,128]{2,1,0:T(8,128)S(1)}, f32[9,56,128]{2,1,0:T(8,128)}, u32[]{:S(2)}) copy-start(f32[9,56,128]{2,1,0:T(8,128)} %param.12) | copy-start | bytes 774148
  106.9 9.0 %copy-start.5 = (f32[9,56,128]{2,1,0:T(8,128)S(1)}, f32[9,56,128]{2,1,0:T(8,128)}, u32[]{:S(2)}) copy-start(f32[9,56,128]{2,1,0:T(8,128)} %copy-done.4) | copy-start | bytes 774148
  106.9 9.0 %copy-start.7 = (f32[9,56,128]{2,1,0:T(8,128)S(1)}, f32[9,56,128]{2,1,0:T(8,128)}, u32[]{:S(2)}) copy-start(f32[9,56,128]{2,1,0:T(8,128)} %copy-done.6) | copy-start | bytes 774148
  107.0 9.0 %copy-start.9 = (f32[9,56,128]{2,1,0:T(8,128)S(1)}, f32[9,56,128]{2,1,0:T(8,128)}, u32[]{:S(2)}) copy-start(f32[9,56,128]{2,1,0:T(8,128)} %copy-done.8) | copy-start | bytes 774148
  107.0 9.0 %copy-start.11 = (f32[9,56,128]{2,1,0:T(8,128)S(1)}, f32[9,56,128]{2,1,0:T(8,128)}, u32[]{:S(2)}) copy-start(f32[9,56,128]{2,1,0:T(8,128)} %copy-done.10) | copy-start | bytes 774148
  107.0 9.0 %copy-start.16 = (f32[9,56,128]{2,1,0:T(8,128)S(1)}, f32[9,56,128]{2,1,0:T(8,128)}, u32[]{:S(2)}) copy-start(f32[9,56,128]{2,1,0:T(8,128)} %copy-done.15) | copy-start | bytes 774148
  109.3 8.7 %copy-start.25 = (s32[64]{0:T(128)S(1)}, s32[64]{0:T(128)}, u32[]{:S(2)}) copy-start(s32[64]{0:T(128)} %param.22) | copy-start | bytes 772
  109.3 8.7 %copy-start.26 = (s32[64]{0:T(128)S(1)}, s32[64]{0:T(128)}, u32[]{:S(2)}) copy-start(s32[64]{0:T(128)} %param.23) | copy-start | bytes 772
  115.9 4.7 %copy-start.21 = (f32[9,9]{1,0:T(8,128)S(1)}, f32[9,9]{1,0:T(8,128)}, u32[]{:S(2)}) copy-start(f32[9,9]{1,0:T(8,128)} %param.16) | copy-start | bytes 976
  116.0 5.4 %copy-start.17 = (f32[512,189]{1,0:T(8,128)S(1)}, f32[512,189]{1,0:T(8,128)}, u32[]{:S(2)}) copy-start(f32[512,189]{1,0:T(8,128)} %gather_fusion.5) | copy-start | bytes 1161220
  132.8 4.4 %copy-start.19 = (f32[256,189]{1,0:T(8,128)S(1)}, f32[256,189]{1,0:T(8,128)}, u32[]{:S(2)}) copy-start(f32[256,189]{1,0:T(8,128)} %copy.227) | copy-start | bytes 580612
  132.8 6.8 %copy-start.18 = (f32[189,512]{1,0:T(8,128)S(1)}, f32[189,512]{1,0:T(8,128)}, u32[]{:S(2)}) copy-start(f32[189,512]{1,0:T(8,128)} %reshape.215) | copy-start | bytes 1161220
  135.0 4.7 %copy-start.22 = (f32[9,9]{1,0:T(8,128)S(1)}, f32[9,9]{1,0:T(8,128)}, u32[]{:S(2)}) copy-start(f32[9,9]{1,0:T(8,128)} %param.17) | copy-start | bytes 976
where the time goes:
time: 144 us; the launch traced here: 142 us
  local copies, waits for them, and re-layouts  95.7 us (66%)
  other arithmetic  20.9 us (15%)
  matrix products  12.5 us (9%)
  starting transfers between devices  11.9 us (8%)
    gather x12, local copies, waits for them, and re-layouts, shards(): sent.append(faces[:, send_slots])  43 us
    unnamed x74, local copies, waits for them, and re-layouts  15.4 us
    gather x6, local copies, waits for them, and re-layouts, shards(): faces[:, flat_neighbour]  13.4 us
    ppermute x4, starting transfers between devices, shifted(): lax.ppermute(value, axis, [(source, source + steps) for source in range(f...  11.9 us
    scatter-add x4, other arithmetic, shards(): outer = outer.at[:, receive_slots[direction]].add(arrived)  8.68 us
    reshape x6, local copies, waits for them, and re-layouts, on_faces(): return faces.reshape(FIELDS * FACE_MODES, -1)  7.31 us
    gather x1, local copies, waits for them, and re-layouts, shards(): target_level = rate_level[receive_slots % count]  6.57 us
    add x4, other arithmetic, weigh_stack(): arrived = arrived + terms[degree][None, :] * stack[degree]  5.7 us
  transfers between devices with their start and end apart: 4, of which 0 were waited for; matrix products, arithmetic and copies ran while one was open for 23% of the time, Pallas kernels for 0%

commit v1 on v0

v1 whole, which is shorter than its diff:
```python
import functools

import jax
import jax.numpy as jnp
from jax import lax
from jax.experimental import pallas as pl
from jax.experimental.pallas import tpu as pltpu
from jax.sharding import PartitionSpec as P

ORDER = 6
LEVELS = 3
coarse_dt = 2.0
slip_keep = 0.3
MESH = pl.DeviceIdType.MESH
F32 = jnp.float32
BF16 = jnp.bfloat16


def up(value, unit):
    return -(-value // unit) * unit


def split(value):
    high = value.astype(BF16)
    return high, (value - high.astype(F32)).astype(BF16)


def dot(left, right):
    return jnp.dot(left, right, preferred_element_type=F32)


def dot_nt(left, right):
    return lax.dot_general(left, right, (((1,), (1,)), ((), ())), preferred_element_type=F32)


def one_hot_columns(row, count):
    where = lax.broadcasted_iota(jnp.int32, (count, row.shape[1]), 0)
    return jnp.where(where == row, 1.0, 0.0).astype(BF16)


def triple(weights, pad):
    high, low = split(weights)
    depth = weights.shape[1]
    row = lax.broadcasted_iota(jnp.int32, (depth, 3 * pad), 0)
    column = lax.broadcasted_iota(jnp.int32, (depth, 3 * pad), 1)
    outer_parts = jnp.where((column == row) | (column == row + 2 * pad), 1.0, 0.0).astype(BF16)
    middle = jnp.where(column == row + pad, 1.0, 0.0).astype(BF16)
    return (dot(high, outer_parts) + dot(low, middle)).astype(BF16)


def kernel(
    sizes,
    state, star, stiffness, project, flux_inner, flux_outer, rate, neighbour, send, receive, fault, slip,
    out,
    current, modal, stacked, stacked_level, integral, projected, padded, faces, outer, lifted, base,
    my_level, their_level, outgoing, incoming,
    level_sent, level_got, data_sent, data_got,
):
    gx_count, gy_count = sizes
    fields, modes, count = state.shape
    face_modes = project.shape[1]
    slots = send.shape[1]
    pad = stacked.shape[0] // 3
    face_pad = up(face_modes, 8)
    rows = projected.shape[0] // (2 * LEVELS)
    gx, gy = lax.axis_index("gx"), lax.axis_index("gy")
    below_x, above_x = gx > 0, gx < gx_count - 1
    below_y, above_y = gy > 0, gy < gy_count - 1
    before_x, after_x = (gx - 1, gy), (gx + 1, gy)
    before_y, after_y = (gx, gy - 1), (gx, gy + 1)
    sources = ((below_x, before_x), (above_x, after_x), (below_y, before_y), (above_y, after_y))
    targets = ((above_x, after_x), (below_x, before_x), (above_y, after_y), (below_y, before_y))

    their_level[...] = jnp.zeros_like(their_level)
    incoming[...] = jnp.zeros_like(incoming)
    barrier = pltpu.get_barrier_semaphore()
    for exists, device in sources:
        @pl.when(exists)
        def _():
            pl.semaphore_signal(barrier, inc=1, device_id=device, device_id_type=MESH)
    rate_row = rate[...]
    rate_rows = jnp.broadcast_to(rate_row.astype(F32), (8, count)).astype(BF16)
    for r in range(4):
        element = receive[r : r + 1, :] & (count - 1) if count & (count - 1) == 0 else receive[r : r + 1, :] % count
        my_level[r] = dot(rate_rows, one_hot_columns(element, count))
    expected = sum(exists.astype(jnp.int32) for exists, _ in sources)
    pl.semaphore_wait(barrier, expected)

    def level_copy(r, device):
        return pltpu.make_async_remote_copy(
            src_ref=my_level.at[r], dst_ref=their_level.at[r],
            send_sem=level_sent.at[r], recv_sem=level_got.at[r],
            device_id=device, device_id_type=MESH,
        )

    def data_copy(r, device):
        return pltpu.make_async_remote_copy(
            src_ref=outgoing.at[r], dst_ref=incoming.at[r],
            send_sem=data_sent.at[r], recv_sem=data_got.at[r],
            device_id=device, device_id_type=MESH,
        )

    for r in range(4):
        exists, device = sources[r]

        @pl.when(exists)
        def _():
            level_copy(r, device).start()

    padded[...] = jnp.zeros_like(padded)
    lifted[...] = jnp.zeros_like(lifted)
    projected[...] = jnp.zeros_like(projected)
    faces[...] = jnp.zeros_like(faces)
    for f in range(4):
        padded[f * face_pad : f * face_pad + face_modes, :] = project[f]
    face_weights = padded[...]
    derive_weights = triple(jnp.concatenate([stiffness[d] for d in range(3)], axis=0), pad)
    project_weights = triple(face_weights, pad)

    def stack_parts(target, column, value):
        grown = jnp.concatenate([value, jnp.zeros((pad - modes, count), F32)], axis=0)
        high, low = split(grown)
        at = slice(column, column + count)
        target[0:pad, at] = high
        target[pad : 2 * pad, at] = high
        target[2 * pad : 3 * pad, at] = low

    def star_sum(use):
        for first in range(0, fields, 3):
            group = range(first, min(first + 3, fields))
            totals = [None] * len(group)
            for d in range(3):
                for q in range(fields):
                    part = modal[d * modes : (d + 1) * modes, q * count : (q + 1) * count]
                    for i, p in enumerate(group):
                        term = star[d, q, p : p + 1, :] * part
                        totals[i] = term if totals[i] is None else totals[i] + term
            for i, p in enumerate(group):
                use(p, totals[i])

    steps = [coarse_dt * 0.5**level for level in range(LEVELS)]
    for q in range(fields):
        stack_parts(stacked, q * count, state[q])
        for level in range(LEVELS):
            integral[level, q] = steps[level] * state[q]

    def taylor(degree, factors):
        scale = 1.0 / (degree.astype(F32) + 2.0)
        factors = [factor * (step * scale) for factor, step in zip(factors, steps)]
        modal[0 : 3 * modes, :] = dot(derive_weights, stacked[...])

        def use(p, total):
            value = -total
            stack_parts(stacked, p * count, value)
            for level in range(LEVELS):
                integral[level, p] += factors[level] * value

        star_sum(use)
        return tuple(factors)

    lax.fori_loop(0, ORDER - 1, taylor, tuple(jnp.float32(step) for step in steps))

    width = fields * count
    for level in range(LEVELS):
        for q in range(fields):
            stack_parts(stacked_level, level * width + q * count, integral[level, q])
    for level in range(LEVELS):
        result = dot(project_weights, stacked_level[:, level * width : (level + 1) * width])
        for f in range(4):
            for q in range(fields):
                faces[q * face_modes : (q + 1) * face_modes, f * count : (f + 1) * count] = (
                    result[f * face_pad : f * face_pad + face_modes, q * count : (q + 1) * count]
                )
        high, low = split(faces[...])
        projected[level * rows : (level + 1) * rows, :] = high
        projected[(LEVELS + level) * rows : (LEVELS + level + 1) * rows, :] = low

    def gather(index_row, level_row):
        found = dot(projected[...], one_hot_columns(index_row, 4 * count))
        total = jnp.zeros((rows, index_row.shape[1]), F32)
        for level in range(LEVELS):
            both = found[level * rows : (level + 1) * rows] + found[(LEVELS + level) * rows : (LEVELS + level + 1) * rows]
            total = jnp.where(level_row == level, both, total)
        return total

    for r in (2, 3, 0, 1):
        exists, device = targets[r]

        @pl.when(exists)
        def _():
            level_copy(r, device).wait_recv()
        outgoing[r] = gather(send[r : r + 1, :], their_level[r][0:1, :])

        @pl.when(exists)
        def _():
            data_copy(r, device).start()

    for f in range(4):
        outer[:, f * count : (f + 1) * count] = gather(neighbour[f : f + 1, :], rate_row)

    own = jnp.zeros((1, 1), F32)
    for q in range(fields):
        own = integral[0, q]
        for level in range(1, LEVELS):
            own = jnp.where(rate_row == level, integral[level, q], own)
        stack_parts(stacked, q * count, own)
    own_lift = lax.dot_general(
        face_weights, face_weights, (((0,), (0,)), ((), ())),
        precision=lax.Precision.HIGHEST, preferred_element_type=F32,
    )
    volume_weights = triple(jnp.concatenate([stiffness[d].T for d in range(3)] + [own_lift], axis=0), pad)
    modal[...] = dot(volume_weights, stacked[...])

    def own_flux(p, total):
        total = total + state[p]
        for q in range(fields):
            total = total + flux_inner[q, p] * modal[3 * modes : 4 * modes, q * count : (q + 1) * count]
        base[p] = total

    star_sum(own_flux)

    slide = dot_nt(
        jnp.broadcast_to(slip[...].astype(F32), (8, slip.shape[1])).astype(BF16),
        one_hot_columns(fault[...], 4 * count),
    )[0:1, :]
    slow = 1.0 - (1.0 - slip_keep) * slide

    for r in (0, 1, 2, 3):
        exists, device = sources[r]

        @pl.when(exists)
        def _():
            data_copy(r, device).wait_recv()
        hot = one_hot_columns(receive[r : r + 1, :], 4 * count)
        high, low = split(incoming[r])
        outer[...] += dot_nt(high, hot) + dot_nt(low, hot)

    for q in range(fields):
        for f in range(4):
            part = outer[q * face_modes : (q + 1) * face_modes, f * count : (f + 1) * count]
            if 3 <= q < 6:
                part = part * slow[:, f * count : (f + 1) * count]
            lifted[f * face_pad : f * face_pad + face_modes, q * count : (q + 1) * count] = part
    lift_high, lift_low = split(face_weights.T)
    high, low = split(lifted[...])
    raised = dot(lift_high, high) + dot(lift_low, high) + dot(lift_high, low)
    for p in range(fields):
        total = base[p]
        for q in range(fields):
            total = total + flux_outer[q, p] * raised[:, q * count : (q + 1) * count]
        out[p] = total

    for r in range(4):
        source_exists, source = sources[r]
        target_exists, target = targets[r]

        @pl.when(source_exists)
        def _():
            level_copy(r, source).wait_send()

        @pl.when(target_exists)
        def _():
            data_copy(r, target).wait_send()


def shards(
    sizes,
    state, star_matrices, stiffness, face_project, flux_inner, flux_outer,
    rate_level, neighbour, send_slots, receive_slots, fault_faces, slip_flags,
):
    fields, modes, count = state.shape
    face_modes = face_project.shape[1]
    slots = send_slots.shape[1]
    pad = up(modes, 16)
    face_pad = up(face_modes, 8)
    rows = up(fields * face_modes, 16)
    width = fields * count
    vmem = pl.BlockSpec(memory_space=pltpu.VMEM)
    smem = pl.BlockSpec(memory_space=pltpu.SMEM)
    return pl.pallas_call(
        functools.partial(kernel, sizes),
        out_shape=jax.ShapeDtypeStruct(state.shape, F32),
        in_specs=[vmem] * 4 + [smem] * 2 + [vmem] * 6,
        out_specs=vmem,
        scratch_shapes=[
            pltpu.VMEM((8, 128), F32),
            pltpu.VMEM((4 * modes, width), F32),
            pltpu.VMEM((3 * pad, width), BF16),
            pltpu.VMEM((3 * pad, LEVELS * width), BF16),
            pltpu.VMEM((LEVELS, fields, modes, count), F32),
            pltpu.VMEM((2 * LEVELS * rows, 4 * count), BF16),
            pltpu.VMEM((4 * face_pad, modes), F32),
            pltpu.VMEM((rows, 4 * count), F32),
            pltpu.VMEM((rows, 4 * count), F32),
            pltpu.VMEM((4 * face_pad, width), F32),
            pltpu.VMEM((fields, modes, count), F32),
            pltpu.VMEM((4, 8, slots), F32),
            pltpu.VMEM((4, 8, slots), F32),
            pltpu.VMEM((4, rows, slots), F32),
            pltpu.VMEM((4, rows, slots), F32),
            pltpu.SemaphoreType.DMA((4,)),
            pltpu.SemaphoreType.DMA((4,)),
            pltpu.SemaphoreType.DMA((4,)),
            pltpu.SemaphoreType.DMA((4,)),
        ],
        compiler_params=pltpu.CompilerParams(
            collective_id=0, has_side_effects=True, vmem_limit_bytes=48 * 1024 * 1024
        ),
    )(
        state, star_matrices, stiffness, face_project, flux_inner, flux_outer,
        rate_level.reshape(1, -1), neighbour, send_slots, receive_slots,
        fault_faces.reshape(1, -1), slip_flags.reshape(1, -1),
    )


def solution(mesh):
    both = ("gx", "gy")
    placed = (
        P(None, None, both), P(None, None, None, both), P(), P(), P(), P(),
        P(both), P(None, both), P(None, both), P(None, both), P(both), P(both),
    )
    sizes = (mesh.shape["gx"], mesh.shape["gy"])
    return jax.shard_map(
        functools.partial(shards, sizes), mesh=mesh, in_specs=placed,
        out_specs=P(None, None, both), check_vma=False,
    )
```

time: 144 us -> 21.7 us (0.15); the launches traced: 142 us -> 21.6 us
  local copies, waits for them, and re-layouts: 95.7 us -> 2.6 us
  other arithmetic: 20.9 us -> 0 us
  Pallas kernels: 0 us -> 18.8 us
  matrix products: 12.5 us -> 0 us
  starting transfers between devices: 11.9 us -> 0 us
    gather x19 -> x0, local copies, waits for them, and re-layouts: 62.9 us -> none  [the longest x12 43 us: shards(): sent.append(faces[:, send_slots])]
    pallas_call x0 -> x1, Pallas kernels: none -> 18.8 us  [shards(): pl.pallas_call(functools.partial(kernel, sizes), out_shape=jax.ShapeDtype...]
    unnamed x74 -> x23, local copies, waits for them, and re-layouts: 15.4 us -> 2.6 us
    dot_general x16 -> x0, matrix products: 12.5 us -> none  [the longest x5 5.09 us: derive(): jnp.einsum('dmn,qne->dqme', stiffness, current, precision=lax.Precision.H...]
    ppermute x4 -> x0, starting transfers between devices: 11.9 us -> none  [shifted(): lax.ppermute(value, axis, [(source, source + steps) for source in range(f...]
    scatter-add x4 -> x0, other arithmetic: 8.68 us -> none  [shards(): outer = outer.at[:, receive_slots[direction]].add(arrived)]
    reshape x8 -> x0, local copies, waits for them, and re-layouts: 8.19 us -> none  [the longest x6 7.31 us: on_faces(): return faces.reshape(FIELDS * FACE_MODES, -1)]
    add x6 -> x0, other arithmetic: 8.02 us -> none  [the longest x4 5.7 us: weigh_stack(): arrived = arrived + terms[degree][None, :] * stack[degree]]
  transfers between devices with their start and end apart: 4 -> 0, of which waited for: 0 -> 0; matrix products, arithmetic and copies ran while one was open for 23% -> 0% of each run, Pallas kernels for 0% -> 0%
where the time goes in v1:
time: 21.7 us; the launch traced here: 21.6 us
  Pallas kernels  18.8 us (87%)
  local copies, waits for them, and re-layouts  2.6 us (12%)
    pallas_call x1, Pallas kernels, shards(): pl.pallas_call(functools.partial(kernel, sizes), out_shape=jax.ShapeDtype...  18.8 us
    unnamed x23, local copies, waits for them, and re-layouts  2.6 us

profile of v1, /device:TPU:1, one launch (start us, length us, event | category | flops | bytes accessed | tf_op | source)
XLA Modules:
  0.0 21.6 jit_solution(1881211489649370757)
XLA Ops:
  0.0 0.0 copy-start
  0.0 0.8 %copy.14.project = f32[4,21,56]{2,1,0:T(8,128)S(1)} copy(f32[4,21,56]{2,0,1:T(4,128)} %param.15) | data formatting | bytes 37632 | tf_op args[3]
  0.8 0.0 copy-start.1
  0.8 0.0 copy-start.2
  0.8 0.0 copy-start.3
  0.9 0.0 copy-start.4
  0.9 0.0 copy-start.5
  0.9 0.0 copy-start.6
  0.9 0.0 copy-start.7
  0.9 0.0 copy-start.8
  0.9 0.0 copy-start.9
  0.9 1.0 %copy.13.star = f32[3,9,9,128]{3,2,1,0:T(8,128)S(1)} copy(f32[3,9,9,128]{3,0,2,1:T(4,128)} %param.13) | data formatting | bytes 248832 | tf_op args[1]
  1.9 0.0 copy-done
  2.0 0.0 copy-done.1
  2.0 0.0 copy-done.2
  2.0 0.0 copy-done.3
  2.0 0.0 copy-done.4
  2.0 0.0 copy-done.5
  2.0 0.0 copy-done.6
  2.0 0.0 copy-done.7
  2.0 0.0 copy-done.8
  2.0 0.0 copy-done.9
  2.0 18.8 %shard_map.118 = f32[9,56,128]{2,1,0:T(8,128)S(1)} custom-call(f32[9,56,128]{2,1,0:T(8,128)S(1)} %copy-done, f32[3,9,9,128]{3,2,1,0:T(8,128)S(1)} %copy.13.star, f32[3,56,56]{2,1,0:T(8,128)S(1)} %copy-done.1, f32[4,21,56]{2,1,0:T(8,128)S(1)} %copy.14.project, f32[9,9]{1,0:T(8,128)S(1)} %copy-done.2, f32[9,9]{1,0:T(8,128)S(1)} %copy-done.3, ...), custom_call_target="tpu_custom_call" | custom-call | tf_op jit(solution)/shard_map/pallas_call | solution.py:280
  20.9 0.7 %copy.16 = f32[9,56,128]{2,1,0:T(8,128)} copy(f32[9,56,128]{2,1,0:T(8,128)S(1)} %shard_map.118) | data formatting | bytes 516096
Async XLA Ops:
  0.0 1.9 %copy-start = (f32[9,56,128]{2,1,0:T(8,128)S(1)}, f32[9,56,128]{2,1,0:T(8,128)}, u32[]{:S(2)}) copy-start(f32[9,56,128]{2,1,0:T(8,128)} %state.1) | copy-start | bytes 774148
  0.8 1.1 %copy-start.1 = (f32[3,56,56]{2,1,0:T(8,128)S(1)}, f32[3,56,56]{2,1,0:T(8,128)}, u32[]{:S(2)}) copy-start(f32[3,56,56]{2,1,0:T(8,128)} %stiffness.1) | copy-start | bytes 112900
  0.8 1.1 %copy-start.2 = (f32[9,9]{1,0:T(8,128)S(1)}, f32[9,9]{1,0:T(8,128)}, u32[]{:S(2)}) copy-start(f32[9,9]{1,0:T(8,128)} %flux_inner.1) | copy-start | bytes 976
  0.8 1.1 %copy-start.3 = (f32[9,9]{1,0:T(8,128)S(1)}, f32[9,9]{1,0:T(8,128)}, u32[]{:S(2)}) copy-start(f32[9,9]{1,0:T(8,128)} %flux_outer.1) | copy-start | bytes 976
  0.9 1.1 %copy-start.4 = (s32[4,256]{1,0:T(4,128)S(1)}, s32[4,256]{1,0:T(4,128)}, u32[]{:S(2)}) copy-start(s32[4,256]{1,0:T(4,128)} %send.1) | copy-start | bytes 12292
  0.9 1.1 %copy-start.5 = (s32[4,256]{1,0:T(4,128)S(1)}, s32[4,256]{1,0:T(4,128)}, u32[]{:S(2)}) copy-start(s32[4,256]{1,0:T(4,128)} %receive.1) | copy-start | bytes 12292
  0.9 1.1 %copy-start.6 = (s32[4,128]{1,0:T(4,128)S(1)}, s32[4,128]{1,0:T(4,128)}, u32[]{:S(2)}) copy-start(s32[4,128]{1,0:T(4,128)} %neighbour.1) | copy-start | bytes 6148
  0.9 1.1 %copy-start.7 = (s32[128]{0:T(128)S(1)}, s32[128]{0:T(128)}, u32[]{:S(2)}) copy-start(s32[128]{0:T(128)} %param.18) | copy-start | bytes 1540
  0.9 1.1 %copy-start.8 = (s32[64]{0:T(128)S(1)}, s32[64]{0:T(128)}, u32[]{:S(2)}) copy-start(s32[64]{0:T(128)} %param.22) | copy-start | bytes 772
  0.9 1.1 %copy-start.9 = (s32[64]{0:T(128)S(1)}, s32[64]{0:T(128)}, u32[]{:S(2)}) copy-start(s32[64]{0:T(128)} %param.23) | copy-start | bytes 772

commit v2 on v1

--- a/solution.py
+++ b/solution.py
@@ -50,15 +50,23 @@
 
 def kernel(
     sizes,
-    state, star, stiffness, project, flux_inner, flux_outer, rate, neighbour, send, receive, fault, slip,
+    state_hbm, star_hbm, stiffness_hbm, project_hbm, flux_inner_hbm, flux_outer_hbm, rate_hbm, neighbour_hbm, send_hbm, receive_hbm,
+    fault_hbm, slip_hbm,
     out,
-    current, modal, stacked, stacked_level, integral, projected, padded, faces, outer, lifted, base,
+    state, star, stiffness, project, flux_inner, flux_outer, rate, neighbour, send, receive, fault, slip, loaded,
+    modal, stacked, stacked_level, integral, projected, padded, faces, outer, lifted, base,
     my_level, their_level, outgoing, incoming,
     level_sent, level_got, data_sent, data_got,
 ):
     gx_count, gy_count = sizes
+    given = (receive_hbm, rate_hbm, stiffness_hbm, project_hbm, state_hbm, star_hbm, send_hbm, neighbour_hbm, fault_hbm, slip_hbm,
+             flux_inner_hbm, flux_outer_hbm)
+    held = (receive, rate, stiffness, project, state, star, send, neighbour, fault, slip, flux_inner, flux_outer)
+    loads = [pltpu.make_async_copy(source, target, loaded.at[i]) for i, (source, target) in enumerate(zip(given, held))]
+    for load in loads:
+        load.start()
     fields, modes, count = state.shape
-    face_modes = project.shape[1]
+    face_modes = project.shape[0]
     slots = send.shape[1]
     pad = stacked.shape[0] // 3
     face_pad = up(face_modes, 8)
@@ -78,11 +86,23 @@
         @pl.when(exists)
         def _():
             pl.semaphore_signal(barrier, inc=1, device_id=device, device_id_type=MESH)
+    loads[0].wait()
+    loads[1].wait()
     rate_row = rate[...]
     rate_rows = jnp.broadcast_to(rate_row.astype(F32), (8, count)).astype(BF16)
     for r in range(4):
         element = receive[r : r + 1, :] & (count - 1) if count & (count - 1) == 0 else receive[r : r + 1, :] % count
         my_level[r] = dot(rate_rows, one_hot_columns(element, count))
+    padded[...] = jnp.zeros_like(padded)
+    lifted[...] = jnp.zeros_like(lifted)
+    faces[fields * face_modes - face_modes :, :] = jnp.zeros((rows - (fields - 1) * face_modes, 4 * count), F32)
+    loads[2].wait()
+    loads[3].wait()
+    for f in range(4):
+        padded[f * face_pad : f * face_pad + face_modes, :] = project[:, f, :]
+    face_weights = padded[...]
+    derive_weights = triple(jnp.concatenate([stiffness[d] for d in range(3)], axis=0), pad)
+    project_weights = triple(face_weights, pad)
     expected = sum(exists.astype(jnp.int32) for exists, _ in sources)
     pl.semaphore_wait(barrier, expected)
 
@@ -107,15 +127,8 @@
         def _():
             level_copy(r, device).start()
 
-    padded[...] = jnp.zeros_like(padded)
-    lifted[...] = jnp.zeros_like(lifted)
-    projected[...] = jnp.zeros_like(projected)
-    faces[...] = jnp.zeros_like(faces)
-    for f in range(4):
-        padded[f * face_pad : f * face_pad + face_modes, :] = project[f]
-    face_weights = padded[...]
-    derive_weights = triple(jnp.concatenate([stiffness[d] for d in range(3)], axis=0), pad)
-    project_weights = triple(face_weights, pad)
+    for load in loads[4:]:
+        load.wait()
 
     def stack_parts(target, column, value):
         grown = jnp.concatenate([value, jnp.zeros((pad - modes, count), F32)], axis=0)
@@ -133,7 +146,7 @@
                 for q in range(fields):
                     part = modal[d * modes : (d + 1) * modes, q * count : (q + 1) * count]
                     for i, p in enumerate(group):
-                        term = star[d, q, p : p + 1, :] * part
+                        term = star[q, p, d : d + 1, :] * part
                         totals[i] = term if totals[i] is None else totals[i] + term
             for i, p in enumerate(group):
                 use(p, totals[i])
@@ -183,20 +196,28 @@
             total = jnp.where(level_row == level, both, total)
         return total
 
-    for r in (2, 3, 0, 1):
-        exists, device = targets[r]
-
-        @pl.when(exists)
-        def _():
-            level_copy(r, device).wait_recv()
-        outgoing[r] = gather(send[r : r + 1, :], their_level[r][0:1, :])
-
-        @pl.when(exists)
-        def _():
-            data_copy(r, device).start()
-
-    for f in range(4):
-        outer[:, f * count : (f + 1) * count] = gather(neighbour[f : f + 1, :], rate_row)
+    for pair in ((2, 3), (0, 1)):
+        for r in pair:
+            exists, device = targets[r]
+
+            @pl.when(exists)
+            def _():
+                level_copy(r, device).wait_recv()
+        index_row = jnp.concatenate([send[r : r + 1, :] for r in pair], axis=1)
+        level_row = jnp.concatenate([their_level[r][0:1, :] for r in pair], axis=1)
+        found = gather(index_row, level_row)
+        for i, r in enumerate(pair):
+            outgoing[r] = found[:, i * slots : (i + 1) * slots]
+        for r in pair:
+            exists, device = targets[r]
+
+            @pl.when(exists)
+            def _():
+                data_copy(r, device).start()
+
+    outer[...] = gather(
+        jnp.concatenate([neighbour[f : f + 1, :] for f in range(4)], axis=1), jnp.concatenate([rate_row] * 4, axis=1)
+    )
 
     own = jnp.zeros((1, 1), F32)
     for q in range(fields):
@@ -276,14 +297,20 @@
     rows = up(fields * face_modes, 16)
     width = fields * count
     vmem = pl.BlockSpec(memory_space=pltpu.VMEM)
-    smem = pl.BlockSpec(memory_space=pltpu.SMEM)
+    hbm = pl.BlockSpec(memory_space=pltpu.HBM)
+    given = (
+        state, star_matrices.transpose(1, 2, 0, 3), stiffness, face_project.transpose(1, 0, 2), flux_inner, flux_outer,
+        rate_level.reshape(1, -1), neighbour, send_slots, receive_slots,
+        fault_faces.reshape(1, -1), slip_flags.reshape(1, -1),
+    )
+    spaces = [pltpu.VMEM] * 4 + [pltpu.SMEM] * 2 + [pltpu.VMEM] * 6
     return pl.pallas_call(
         functools.partial(kernel, sizes),
         out_shape=jax.ShapeDtypeStruct(state.shape, F32),
-        in_specs=[vmem] * 4 + [smem] * 2 + [vmem] * 6,
+        in_specs=[hbm] * 12,
         out_specs=vmem,
-        scratch_shapes=[
-            pltpu.VMEM((8, 128), F32),
+        scratch_shapes=[space(array.shape, array.dtype) for space, array in zip(spaces, given)] + [
+            pltpu.SemaphoreType.DMA((12,)),
             pltpu.VMEM((4 * modes, width), F32),
             pltpu.VMEM((3 * pad, width), BF16),
             pltpu.VMEM((3 * pad, LEVELS * width), BF16),
@@ -304,13 +331,9 @@
             pltpu.SemaphoreType.DMA((4,)),
         ],
         compiler_params=pltpu.CompilerParams(
-            collective_id=0, has_side_effects=True, vmem_limit_bytes=48 * 1024 * 1024
+            collective_id=0, has_side_effects=True, vmem_limit_bytes=64 * 1024 * 1024 - 65536
         ),
-    )(
-        state, star_matrices, stiffness, face_project, flux_inner, flux_outer,
-        rate_level.reshape(1, -1), neighbour, send_slots, receive_slots,
-        fault_faces.reshape(1, -1), slip_flags.reshape(1, -1),
-    )
+    )(*given)
 
 
 def solution(mesh):

time: 21.7 us -> 19.6 us (0.903)
  Pallas kernels: 18.8 us -> 17.8 us
  local copies, waits for them, and re-layouts: 2.6 us -> 1.66 us
    pallas_call x1, Pallas kernels: 18.8 us -> 17.8 us  [shards(): pl.pallas_call(functools.partial(kernel, sizes), out_shape=jax.ShapeDtype...]
    unnamed x23 -> x1, local copies, waits for them, and re-layouts: 2.6 us -> 1.66 us
where the time goes in v2:
time: 19.6 us; the launch traced here: 19.4 us
  Pallas kernels  17.8 us (91%)
  local copies, waits for them, and re-layouts  1.66 us (8%)
    pallas_call x1, Pallas kernels, shards(): pl.pallas_call(functools.partial(kernel, sizes), out_shape=jax.ShapeDtype...  17.8 us
    unnamed x1, local copies, waits for them, and re-layouts  1.66 us

profile of v2, /device:TPU:1, one launch (start us, length us, event | category | flops | bytes accessed | tf_op | source)
XLA Modules:
  0.0 19.4 jit_solution(1980219412519710672)
XLA Ops:
  0.0 17.8 %shard_map.118 = f32[9,56,128]{2,1,0:T(8,128)} custom-call(f32[9,56,128]{2,1,0:T(8,128)} %state_hbm.1, f32[9,9,3,128]{3,2,1,0:T(4,128)} %bitcast.5, f32[3,56,56]{2,1,0:T(8,128)} %stiffness_hbm.1, f32[21,4,56]{2,1,0:T(4,128)} %bitcast.6, f32[9,9]{1,0:T(8,128)} %flux_inner_hbm.1, f32[9,9]{1,0:T(8,128)} %flux_outer_hbm.1, s32[1,128]{1,0:T(1,128)} %bitcast.7, ...), custom_call_target="tpu_custom_call" | custom-call | tf_op jit(solution)/shard_map/pallas_call | solution.py:307
  17.8 1.7 %copy.14 = f32[9,56,128]{2,1,0:T(8,128)} copy(f32[9,56,128]{2,1,0:T(8,128)} %shard_map.118) | data formatting | bytes 516096

commit v3 on v2

--- a/solution.py
+++ b/solution.py
@@ -246,13 +246,16 @@
     )[0:1, :]
     slow = 1.0 - (1.0 - slip_keep) * slide
 
+    hots = [one_hot_columns(receive[r : r + 1, :], 4 * count) for r in range(4)]
+    lift_high, lift_low = split(face_weights.T)
+
     for r in (0, 1, 2, 3):
         exists, device = sources[r]
 
         @pl.when(exists)
         def _():
             data_copy(r, device).wait_recv()
-        hot = one_hot_columns(receive[r : r + 1, :], 4 * count)
+        hot = hots[r]
         high, low = split(incoming[r])
         outer[...] += dot_nt(high, hot) + dot_nt(low, hot)
 
@@ -262,7 +265,6 @@
             if 3 <= q < 6:
                 part = part * slow[:, f * count : (f + 1) * count]
             lifted[f * face_pad : f * face_pad + face_modes, q * count : (q + 1) * count] = part
-    lift_high, lift_low = split(face_weights.T)
     high, low = split(lifted[...])
     raised = dot(lift_high, high) + dot(lift_low, high) + dot(lift_high, low)
     for p in range(fields):

time: 19.6 us -> 19.5 us (level)
  no operation moved by 1% of the time
where the time goes in v3:
time: 19.5 us; the launch traced here: 19.4 us
  Pallas kernels  17.7 us (91%)
  local copies, waits for them, and re-layouts  1.66 us (9%)
    pallas_call x1, Pallas kernels, shards(): pl.pallas_call(functools.partial(kernel, sizes), out_shape=jax.ShapeDtype...  17.7 us
    unnamed x1, local copies, waits for them, and re-layouts  1.66 us

profile of v3, /device:TPU:1, one launch (start us, length us, event | category | flops | bytes accessed | tf_op | source)
XLA Modules:
  0.0 19.4 jit_solution(12542709726970454894)
XLA Ops:
  0.0 17.7 %shard_map.118 = f32[9,56,128]{2,1,0:T(8,128)} custom-call(f32[9,56,128]{2,1,0:T(8,128)} %state_hbm.1, f32[9,9,3,128]{3,2,1,0:T(4,128)} %bitcast.5, f32[3,56,56]{2,1,0:T(8,128)} %stiffness_hbm.1, f32[21,4,56]{2,1,0:T(4,128)} %bitcast.6, f32[9,9]{1,0:T(8,128)} %flux_inner_hbm.1, f32[9,9]{1,0:T(8,128)} %flux_outer_hbm.1, s32[1,128]{1,0:T(1,128)} %bitcast.7, ...), custom_call_target="tpu_custom_call" | custom-call | tf_op jit(solution)/shard_map/pallas_call | solution.py:309
  17.7 1.7 %copy.14 = f32[9,56,128]{2,1,0:T(8,128)} copy(f32[9,56,128]{2,1,0:T(8,128)} %shard_map.118) | data formatting | bytes 516096
